TPU v7x, 768 devices: a whole 4x8x12 slice. The times are simulated.
768 devices in a mesh: row: 12 (over z_hi, x), col: 64 (over y, z_lo, core).
Axes of the slice: x: 4, y: 8, z: 12 (z_hi: 3, z_lo: 4; z = z_hi * 4 + z_lo), core: 2. Of those that a mesh axis runs over, the one named last changes fastest.
Arguments:
- gate_pre: bfloat16 [1536, 26624], P('row', 'col'), may hold values from -16 to 16
- up_pre: bfloat16 [1536, 26624], P('row', 'col'), may hold values from -6 to 6
- down_weight: bfloat16 [26624, 9216], P('col', 'row'), may hold values from -0.0390625 to 0.0390625
- out_grad: bfloat16 [1536, 9216], P('col', 'row'), may hold values from -6 to 6
- noised: int32 [1536], P('col'), may hold values from 0 to 1, as said below
Outputs:
- layer_out: bfloat16 [1536, 9216], P('col', 'row')
- gate_grad: bfloat16 [1536, 26624], P('row', 'col')
- up_grad: bfloat16 [1536, 26624], P('row', 'col')
- weight_grad: bfloat16 [26624, 9216], P('col', 'row')
Inputs may be any that keep to these rules, and one draw needn't show every extreme that they name: Every aligned block of 24 tokens holds at least one noised token.
All inputs are finite; a program needn't handle non-finite values.
Results may differ from a plain program's by a relative error of at most 0.018.
Values may be sent and summed in bfloat16 or wider, within the bound.
A program may use at most 32 MiB of HBM per device.

v0:
```python
import jax
import jax.numpy as jnp
from jax import lax
from jax.sharding import PartitionSpec as P


def swiglu_parts(gate_pre, up_pre):
    gate = gate_pre.astype(jnp.float32)
    upper = up_pre.astype(jnp.float32)
    sigma = jax.nn.sigmoid(gate)
    return (gate, upper, sigma, gate * sigma)


def body(gate_pre, up_pre, down_weight, out_grad, noised):
    gate, upper, sigma, silu_gate = swiglu_parts(gate_pre, up_pre)
    hidden = (silu_gate * upper).astype(jnp.bfloat16)
    gathered = lax.all_gather(hidden, "row", axis=0, tiled=True)
    own_tokens = out_grad.shape[0]
    rows = gathered
    layer_out = lax.psum_scatter(
        jnp.dot(rows, down_weight, preferred_element_type=jnp.float32),
        "col",
        scatter_dimension=0,
        tiled=True,
    ).astype(jnp.bfloat16)
    total = own_tokens * lax.axis_size("col")
    local_flags = noised.astype(jnp.float32)
    count = lax.psum(jnp.sum(local_flags), "col")
    local_scaled = (out_grad.astype(jnp.float32) * local_flags[:, None] * (total / count)).astype(
        jnp.bfloat16
    )
    scaled = lax.all_gather(local_scaled, "col", axis=0, tiled=True)
    rows = scaled
    hidden_grad = lax.psum_scatter(
        lax.dot_general(
            rows, down_weight, (((1,), (1,)), ((), ())), preferred_element_type=jnp.float32
        ).astype(jnp.bfloat16),
        "row",
        scatter_dimension=0,
        tiled=True,
    ).astype(jnp.float32)
    slope = sigma * (1.0 + gate * (1.0 - sigma))
    gate_grad = (hidden_grad * upper * slope).astype(jnp.bfloat16)
    up_grad = (hidden_grad * silu_gate).astype(jnp.bfloat16)
    weight_grad = lax.dot_general(
        gathered, scaled, (((0,), (0,)), ((), ())), preferred_element_type=jnp.float32
    ).astype(jnp.bfloat16)
    return (layer_out, gate_grad, up_grad, weight_grad)


def solution(mesh):
    return jax.shard_map(
        body,
        mesh=mesh,
        in_specs=(P("row", "col"), P("row", "col"), P("col", "row"), P("col", "row"), P("col")),
        out_specs=(P("col", "row"), P("row", "col"), P("row", "col"), P("col", "row")),
        check_vma=False,
    )
```

profile of v0, /device:TPU:1, one launch (start us, length us, event | category | flops | bytes accessed | tf_op | source)
XLA Modules:
  0.0 827.3 jit_solution(9815132794266937313)
XLA Ops:
  7.2 0.0 copy-start
  7.2 0.0 all-gather.5.cloned.1.call-start
  7.2 1.3 convert_reduce_fusion
  8.5 0.7 convert_element_type.41
  9.2 143.9 %psum.7 = f32[]{:T(128)} all-reduce(f32[]{:T(128)} %convert_reduce_fusion), channel_id=1, replica_groups=mesh['row'=12,'col'=64] {'col'}, use_global_device_ids=true, to_apply=%region_2.0 | all-reduce | flops 1 | bytes 8 | tf_op jit(solution)/shard_map/psum | solution.py:28
  153.8 1.5 multiply_convert_fusion
  155.3 0.0 all-gather.5.cloned.1.call-update
  155.3 0.0 reduce-scatter.7.cloned.1.call-start
  155.4 121.7 %all-gather.5.cloned.1.call-done = bf16[1536,768]{1,0:T(8,128)(2,1)} async-done(((bf16[24,768]{1,0:T(8,128)(2,1)}), bf16[1536,768]{1,0:T(8,128)(2,1)}) %all-gather.5.cloned.1.call-update) | async-done | bytes 2359312 | tf_op jit(solution)/shard_map/all_gather | solution.py:32
  277.0 0.0 copy-done
  277.0 2.8 convolution_convert_fusion
  279.9 1.6 copy.9
  281.5 0.0 copy-start.1
  281.5 0.0 copy-start.2
  281.5 0.0 reduce-scatter.7.cloned.1.call-update
  281.5 0.0 all-gather.3.cloned.1.call-start
  281.5 169.7 %reduce-scatter.7.cloned.1.call-done = bf16[128,416]{1,0:T(8,128)(2,1)} async-done(((bf16[1536,416]{1,0:T(8,128)(2,1)}), bf16[128,416]{1,0:T(8,128)(2,1)}) %reduce-scatter.7.cloned.1.call-update) | async-done | bytes 106512
  451.2 1.0 copy.10
  452.2 0.0 copy-done.1
  452.3 0.0 copy-done.2
  452.3 0.8 fusion.3
  453.1 0.0 all-gather.3.cloned.1.call-update
  453.1 0.0 reduce-scatter.5.cloned.1.call-start
  453.2 78.4 %all-gather.3.cloned.1.call-done = bf16[1536,416]{0,1:T(8,128)(2,1)} async-done(((bf16[128,416]{0,1:T(8,128)(2,1)}), bf16[1536,416]{0,1:T(8,128)(2,1)}) %all-gather.3.cloned.1.call-update) | async-done | bytes 1277968 | tf_op jit(solution)/shard_map/all_gather | solution.py:17
  531.6 4.9 fusion.9
  536.4 0.0 copy-start.3
  536.4 0.0 reduce-scatter.5.cloned.1.call-update
  536.4 1.6 copy-done.3
  538.1 3.3 convolution_convert_fusion.1
  541.4 277.9 %reduce-scatter.5.cloned.1.call-done = f32[24,768]{1,0:T(8,128)} async-done(((f32[1536,768]{1,0:T(8,128)}), f32[24,768]{1,0:T(8,128)}) %reduce-scatter.5.cloned.1.call-update) | async-done | bytes 73744 | tf_op jit(solution)/shard_map/reduce_scatter | solution.py:20
  819.2 1.5 convert_element_type.39
Async XLA Ops:
  7.2 269.9 %copy-start = (bf16[416,768]{1,0:T(8,128)(2,1)S(1)}, bf16[416,768]{1,0:T(8,128)(2,1)}, u32[]{:S(2)}) copy-start(bf16[416,768]{1,0:T(8,128)(2,1)} %param.7) | copy-start | bytes 1916932
  7.2 269.9 %all-gather.5.cloned.1.call-start = ((), (), s32[]{:S(2)}) async-start(), calls=%async_computation.4 | async-start | bytes 2396160 | tf_op jit(solution)/shard_map/all_gather | solution.py:32
  155.3 295.9 %reduce-scatter.7.cloned.1.call-start = ((), (), s32[]{:S(2)}) async-start(), calls=%async_computation.5 | async-start | bytes 1703936
  281.5 170.8 %copy-start.1 = (bf16[128,416]{0,1:T(8,128)(2,1)S(1)}, bf16[128,416]{0,1:T(8,128)(2,1)}, u32[]{:S(2)}) copy-start(bf16[128,416]{0,1:T(8,128)(2,1)} %param.5) | copy-start | bytes 319492
  281.5 170.8 %copy-start.2 = (bf16[128,416]{0,1:T(8,128)(2,1)S(1)}, bf16[128,416]{0,1:T(8,128)(2,1)}, u32[]{:S(2)}) copy-start(bf16[128,416]{0,1:T(8,128)(2,1)} %param.6) | copy-start | bytes 319492
  281.5 250.1 %all-gather.3.cloned.1.call-start = ((), (), s32[]{:S(2)}) async-start(), calls=%async_computation.2 | async-start | bytes 1384448 | tf_op jit(solution)/shard_map/all_gather | solution.py:17
  453.1 366.1 %reduce-scatter.5.cloned.1.call-start = ((), (), s32[]{:S(2)}) async-start(), calls=%async_computation.3 | async-start | bytes 4792320 | tf_op jit(solution)/shard_map/reduce_scatter | solution.py:20
  536.4 1.7 copy-start.3
Sparse Core Ops, SparseCore 0:
  155.4 121.5 all-gather.4
  282.3 168.8 reduce-scatter.6
  455.7 75.8 all-gather.2
  536.6 282.6 reduce-scatter.4
where the time goes:
time: 832 us; the launch traced here: 827 us
  waiting for transfers between devices  648 us (78%)
  blocking collectives  144 us (17%)
  between operations  14.5 us (2%)
  matrix products  11 us (1%)
    reduce_scatter x1, waiting for transfers between devices, body(): lax.psum_scatter(jnp.dot(rows, down_weight, preferred_element_type=jnp.fl...  278 us
    unnamed x5, waiting for transfers between devices  170 us
    psum x1, blocking collectives, body(): count = lax.psum(jnp.sum(local_flags), 'col')  144 us
    all_gather x1, waiting for transfers between devices, body(): scaled = lax.all_gather(local_scaled, 'col', axis=0, tiled=True)  122 us
    all_gather x1, waiting for transfers between devices, body(): gathered = lax.all_gather(hidden, 'row', axis=0, tiled=True)  78.4 us
  transfers between devices with their start and end apart: 4, of which 4 were waited for; matrix products, arithmetic and copies ran while one was open for 0% of the time, Pallas kernels for 0%

commit v1 on v0

v1 whole, which is shorter than its diff:
```python
import jax
import jax.numpy as jnp
from jax import lax
from jax.experimental import pallas as pl
from jax.experimental.pallas import tpu as pltpu
from jax.sharding import PartitionSpec as P

MESH = pl.DeviceIdType.MESH
F32 = jnp.float32
BF16 = jnp.bfloat16
NZ, NX, NY, NL = 3, 4, 8, 4
COPIES = 128


def kernel(
    gate_ref, up_ref, w_ref, og_ref, noised_ref,
    lo_ref, gg_ref, ug_ref, wg_ref,
    x0_send, x0_recv, s_buf, ht, h_buf, cl_send, cl_recv, cy_own, cy_recv,
    po, ps, pr, y_send, y_recv, l_send, l_recv, fin, fin_recv,
    gt, x_send, x_recv, z_send, z_recv,
    send_sem, recv_sem,
):
    tok, ff = gate_ref.shape
    own_tok, feat = og_ref.shape
    half = feat // 2
    pair = 2 * own_tok
    group = NL * pair
    tokens = tok * NZ * NX

    row, col = lax.axis_index("row"), lax.axis_index("col")
    zh, x = row // NX, row % NX
    c, chip = col % 2, col // 2
    y, zl = chip // NL, chip % NL
    first = c == 0
    sgn = 1 - 2 * c

    def at(zh_=zh, x_=x, y_=y, zl_=zl, c_=c):
        return (zh_ * NX + x_, (y_ * NL + zl_) * 2 + c_)

    def xi(d):
        return (x + sgn * d + 2 * NX) % NX

    def yi(d):
        return (y + sgn * d + 2 * NY) % NY

    sibling = at(c_=1 - c)
    x_long, x_short = at(x_=xi(1)), at(x_=xi(-1))
    y_long, y_short = at(y_=yi(1)), at(y_=yi(-1))
    zl_at = [at(zl_=(zl + k) % NL) for k in range(NL)]
    zh_at = [at(zh_=(zh + k) % NZ) for k in range(NZ)]

    started = []

    def send(src, dst, device):
        i = len(started)
        copy = pltpu.make_async_remote_copy(
            src_ref=src, dst_ref=dst, send_sem=send_sem.at[i], recv_sem=recv_sem.at[i],
            device_id=device, device_id_type=MESH,
        )
        copy.start()
        started.append(copy)
        return copy

    barrier = pltpu.get_barrier_semaphore()
    partners = [sibling, x_long, x_short, y_long, y_short] + zl_at[1:] + zh_at[1:]
    for partner in partners:
        pl.semaphore_signal(barrier, inc=1, device_id=partner, device_id_type=MESH)

    flags_row = noised_ref[...].astype(F32)
    i0 = lax.broadcasted_iota(jnp.int32, (own_tok, own_tok), 0)
    i1 = lax.broadcasted_iota(jnp.int32, (own_tok, own_tok), 1)
    flags = jnp.sum(
        jnp.where(i0 == i1, jnp.broadcast_to(flags_row, (own_tok, own_tok)), 0.0),
        axis=1, keepdims=True,
    )
    masked = og_ref[...].astype(F32) * flags
    own_count = jnp.sum(jnp.broadcast_to(flags_row, (8, own_tok)), axis=1, keepdims=True)
    lo, hi = masked[:, :half], masked[:, half:]
    x0_send[0:own_tok, :] = jnp.where(first, hi, lo)
    x0_send[own_tok:own_tok + 8, :] = jnp.broadcast_to(own_count, (8, half))
    kept = jnp.where(first, lo, hi)

    pl.semaphore_wait(barrier, len(partners))
    x0 = send(x0_send, x0_recv, sibling)

    def parts():
        gate = gate_ref[...].astype(F32)
        sigma = jax.nn.sigmoid(gate)
        return gate, up_ref[...].astype(F32), sigma, gate * sigma

    _, upper, _, silu = parts()
    ht[row] = jnp.transpose((silu * upper)).astype(BF16)

    hb = ff // 2
    halves = [pl.ds(0, hb), pl.ds(hb, hb)]
    z_cp = [[send(ht.at[row, p], ht.at[row, p], zh_at[k]) for k in (1, 2)] for p in halves]

    def block(k, d):
        return ((zh - k + NZ) % NZ) * NX + xi(d)

    def x_start(k, p):
        b = ht.at[block(k, 0), p]
        return [send(b, b, x_long), send(b, b, x_short)]

    def x_forward(cps, k, p):
        cps[0].wait_recv()
        b = ht.at[block(k, -1), p]
        cps.append(send(b, b, x_long))

    whole = pl.ds(0, ff)
    xa = x_start(0, whole)

    x0.wait_recv()
    got = x0_recv[0:own_tok, :]
    cols = pl.ds(pl.multiple_of(c * half, 128), half)

    def s_block(y_, l_, n=1):
        return s_buf.at[pl.ds(pl.multiple_of((y_ * NL + l_) * pair, 16), n * pair), cols]

    s_block(y, zl)[...] = jnp.concatenate(
        [jnp.where(first, kept, got), jnp.where(first, got, kept)], axis=0
    ).astype(BF16)
    cl_send[...] = own_count + x0_recv[own_tok:own_tok + 8, 0:128]
    own = s_block(y, zl)
    l_cp = [send(own, own, zl_at[k]) for k in range(1, NL)]
    cl_cp = [send(cl_send, cl_recv.at[k - 1], zl_at[k]) for k in range(1, NL)]

    y_cp = {}

    def y_start(k, way, step):
        sign = 1 if way == 0 else -1
        b = s_block(yi(-sign * step), (zl - k + NL) % NL)
        if step:
            y_cp[k, way, step - 1].wait_recv()
        y_cp[k, way, step] = send(b, b, (y_long, y_short)[way])

    y_start(0, 0, 0)
    y_start(0, 1, 0)
    for k in range(1, NL):
        l_cp[k - 1].wait_recv()
        y_start(k, 0, 0)
        y_start(k, 1, 0)
    sib_cp = {}

    def to_sibling(d):
        b = s_block(yi(d), 0, NL)
        sib_cp[d % NY] = send(b, b, sibling)

    to_sibling(0)
    total = cl_send[...]
    for k in range(1, NL):
        cl_cp[k - 1].wait_recv()
        total = total + cl_recv[k - 1]
    cy_own[...] = total
    cy_cp = {}

    def cy_start(way, step):
        if step:
            cy_cp[way, step - 1].wait_recv()
        slot = way * 4 + step
        src = cy_recv.at[slot - 1] if step else cy_own
        cy_cp[way, step] = send(src, cy_recv.at[slot], (y_long, y_short)[way])

    cy_start(0, 0)
    cy_start(1, 0)

    x_forward(xa, 0, whole)
    for k in range(NL):
        y_start(k, 0, 1)
        y_start(k, 1, 1)
    cy_start(0, 1)
    cy_start(1, 1)
    to_sibling(-1)
    to_sibling(1)

    def to_rows(k, d):
        b = block(k, d)
        h_buf[pl.ds(pl.multiple_of(b * tok, tok), tok), :] = jnp.transpose(ht[b])

    to_rows(0, 0)

    xb = []
    for k in (1, 2):
        z_cp[0][k - 1].wait_recv()
        xb.append(x_start(k, halves[0]))
    for k in range(NL):
        y_start(k, 0, 2)
        y_start(k, 1, 2)
    cy_start(0, 2)
    cy_start(1, 2)
    to_sibling(-2)
    to_sibling(2)
    for k in (1, 2):
        x_forward(xb[k - 1], k, halves[0])
    xa[1].wait_recv()
    to_rows(0, -1)
    to_rows(0, 1)
    xc = []
    for k in (1, 2):
        z_cp[1][k - 1].wait_recv()
        xc.append(x_start(k, halves[1]))
    for k in range(NL):
        y_start(k, 0, 3)
    cy_start(0, 3)
    xa[2].wait_recv()
    to_rows(0, 2)
    for k in range(NL):
        y_cp[k, 1, 2].wait_recv()
    to_sibling(-3)
    to_sibling(3)
    for k in (1, 2):
        x_forward(xc[k - 1], k, halves[1])
    to_rows(1, 0)
    to_rows(2, 0)
    for k in range(NL):
        y_cp[k, 0, 3].wait_recv()
    to_sibling(4)
    for k in (1, 2):
        xb[k - 1][1].wait_recv()
        xc[k - 1][1].wait_recv()
        to_rows(k, 1)
        to_rows(k, -1)

    for d in range(NY):
        sib_cp[d].wait_recv()

    span = NX * tok
    pieces = {"A0": (1, 0, hb), "B0": (2, 0, hb), "A1": (1, hb, hb), "B1": (2, hb, hb), "C": (0, 0, ff)}
    g_cp = {}

    def g_product(name):
        k, r0, n = pieces[name]
        other = (zh + k) % NZ
        rows = s_buf[pl.ds(pl.multiple_of(other * span, span), span), :]
        out = lax.dot_general(
            w_ref[r0:r0 + n, :], rows, (((1,), (1,)), ((), ())), preferred_element_type=F32
        )
        for x_ in range(NX):
            d = (sgn * (x_ - x) + 2 * NX) % NX
            gt[k, d, r0:r0 + n, :] = out[:, x_ * tok:(x_ + 1) * tok]

    def g_send(name, slot, value, device):
        k, r0, n = pieces[name]
        x_send[slot, k, r0:r0 + n, :] = value.astype(BF16)
        g_cp[name, slot] = send(
            x_send.at[slot, k, pl.ds(r0, n)], x_recv.at[slot, k, pl.ds(r0, n)], device
        )

    def g_got(name, slot):
        k, r0, n = pieces[name]
        g_cp[name, slot].wait_recv()
        return x_recv[slot, k, r0:r0 + n, :].astype(F32)

    def g_own(name, d):
        k, r0, n = pieces[name]
        return gt[k, d, r0:r0 + n, :]

    def g_first(name):
        g_product(name)
        g_send(name, 0, g_own(name, 2), x_long)
        g_send(name, 1, g_own(name, 3), x_short)

    def g_second(name):
        g_send(name, 2, g_own(name, 1) + g_got(name, 0), x_long)

    zr_cp = {}

    def g_last(name):
        k, r0, n = pieces[name]
        value = g_own(name, 0) + g_got(name, 1) + g_got(name, 2)
        if k == 0:
            return value
        z_send[k - 1, r0:r0 + n, :] = value.astype(BF16)
        zr_cp[name] = send(
            z_send.at[k - 1, pl.ds(r0, n)], z_recv.at[k - 1, pl.ds(r0, n)], zh_at[k]
        )
        return None

    p_cp = {}

    def p_product(d):
        d = d % NY
        out = jnp.dot(
            h_buf[pl.ds(pl.multiple_of(yi(d) * group, 16), group), :], w_ref[...],
            preferred_element_type=F32,
        )
        mine = jnp.where(first, out[:, :half], out[:, half:])
        theirs = jnp.where(first, out[:, half:], out[:, :half]).astype(BF16)
        for a in range(NL):
            slot = (a - zl - 1 + 2 * NL) % NL
            po[d, slot] = mine[a * pair:(a + 1) * pair]
            ps[d, slot] = theirs[a * pair:(a + 1) * pair]
        p_cp[d] = send(ps.at[d], pr.at[(NY - d) % NY], sibling)

    def p_wait(d):
        p_cp[(NY - d) % NY].wait_recv()

    ry_cp = {}

    def p_sum(d, g):
        d = d % NY
        return po[d, 2 * g:2 * g + 2] + pr[d, 2 * g:2 * g + 2].astype(F32)

    def ry_send(way, step, g):
        d = 4 - step if way == 0 else step - 3
        slot = way * 4 + step
        value = p_sum(d, g)
        if step:
            ry_cp[way, step - 1, g].wait_recv()
            value = value + y_recv[slot - 1, 2 * g:2 * g + 2].astype(F32)
        y_send[slot, 2 * g:2 * g + 2] = value.astype(BF16)
        ry_cp[way, step, g] = send(
            y_send.at[slot, pl.ds(2 * g, 2)], y_recv.at[slot, pl.ds(2 * g, 2)],
            (y_long, y_short)[way],
        )

    def ry_last(g):
        ry_cp[0, 3, g].wait_recv()
        ry_cp[1, 2, g].wait_recv()
        return (
            p_sum(0, g) + y_recv[3, 2 * g:2 * g + 2].astype(F32)
            + y_recv[6, 2 * g:2 * g + 2].astype(F32)
        )

    g_first("A0")
    g_first("B0")
    for k in (1, 2):
        xb[k - 1][2].wait_recv()
        xc[k - 1][2].wait_recv()
        to_rows(k, 2)
    p_product(4)
    p_product(3)
    p_product(-3)
    g_first("A1")
    g_first("B1")
    p_wait(4)
    for g in range(2):
        ry_send(0, 0, g)
    p_wait(5)
    for g in range(2):
        ry_send(1, 0, g)
    p_product(2)
    p_product(-2)
    g_second("A0")
    g_second("B0")
    p_product(1)
    p_product(-1)
    g_first("C")
    p_product(0)
    g_second("A1")
    g_second("B1")
    p_wait(3)
    p_wait(6)
    for g in range(2):
        ry_send(0, 1, g)
        ry_send(1, 1, g)
    g_last("A0")
    g_last("B0")
    for d in (2, 7):
        p_wait(d)
    for g in range(2):
        ry_send(0, 2, g)
        ry_send(1, 2, g)
    g_last("A1")
    g_last("B1")
    g_second("C")

    for way in range(2):
        cy_cp[way, 3 - way].wait_recv()
    count = cy_own[...]
    for slot in range(7):
        count = count + cy_recv[slot]
    scale = tokens / count

    nb = 256
    scale_w = jnp.broadcast_to(scale[0:1, 0:1], (1, nb))

    def w_product(j):
        acc = jnp.zeros((ff, nb), F32)
        for i in range(NZ * NX // 2):
            acc = acc + jnp.dot(
                jnp.concatenate([ht[2 * i], ht[2 * i + 1]], axis=1),
                s_buf[2 * tok * i:2 * tok * (i + 1), j * nb:(j + 1) * nb],
                preferred_element_type=F32,
            )
        wg_ref[:, j * nb:(j + 1) * nb] = (acc * scale_w).astype(BF16)

    w_product(0)
    for d in (1, 0):
        p_wait(d)
    for g in range(2):
        ry_send(0, 3, g)
    w_product(1)
    w_product(2)
    tail = g_last("C")
    fl_cp = []
    v0 = ry_last(0)
    for j in range(2):
        l_send[j] = v0[j].astype(BF16)
        fl_cp.append(send(l_send.at[j], l_recv.at[j], zl_at[j + 1]))
    v1 = ry_last(1)
    l_send[2] = v1[0].astype(BF16)
    fl_cp.append(send(l_send.at[2], l_recv.at[2], zl_at[3]))
    out = v1[1]
    for j in range(3):
        fl_cp[j].wait_recv()
        out = out + l_recv[j].astype(F32)
    fin[0] = out[:own_tok]
    fin[1] = out[own_tok:]
    fin_cp = send(fin.at[1 - c], fin_recv, sibling)

    for cp in zr_cp.values():
        cp.wait_recv()
    grad = jnp.transpose(tail + z_recv[0].astype(F32) + z_recv[1].astype(F32))
    grad = grad * jnp.broadcast_to(scale[0:1, 0:1], (1, ff))
    gate, upper, sigma, silu = parts()
    gg_ref[...] = (grad * upper * (sigma * (1.0 + gate * (1.0 - sigma)))).astype(BF16)
    ug_ref[...] = (grad * silu).astype(BF16)

    fin_cp.wait_recv()
    mine, theirs = fin[c], fin_recv[...]
    lo_ref[:, :half] = jnp.where(first, mine, theirs).astype(BF16)
    lo_ref[:, half:] = jnp.where(first, theirs, mine).astype(BF16)
    for copy in started:
        copy.wait_send()


def body(gate_pre, up_pre, down_weight, out_grad, noised):
    tok, ff = gate_pre.shape
    own, feat = out_grad.shape
    half, pair, tokens = feat // 2, 2 * own, tok * NZ * NX
    vmem = pl.BlockSpec(memory_space=pltpu.VMEM)
    return pl.pallas_call(
        kernel,
        out_shape=(
            jax.ShapeDtypeStruct((own, feat), BF16),
            jax.ShapeDtypeStruct((tok, ff), BF16),
            jax.ShapeDtypeStruct((tok, ff), BF16),
            jax.ShapeDtypeStruct((ff, feat), BF16),
        ),
        in_specs=[vmem] * 5,
        out_specs=(vmem,) * 4,
        scratch_shapes=[
            pltpu.VMEM((own + 8, half), F32),
            pltpu.VMEM((own + 8, half), F32),
            pltpu.VMEM((tokens, feat), BF16),
            pltpu.VMEM((NZ * NX, ff, tok), BF16),
            pltpu.VMEM((tokens, ff), BF16),
            pltpu.VMEM((8, 128), F32),
            pltpu.VMEM((NL - 1, 8, 128), F32),
            pltpu.VMEM((8, 128), F32),
            pltpu.VMEM((NY - 1, 8, 128), F32),
            pltpu.VMEM((NY, NL, pair, half), F32),
            pltpu.VMEM((NY, NL, pair, half), BF16),
            pltpu.VMEM((NY, NL, pair, half), BF16),
            pltpu.VMEM((NY - 1, NL, pair, half), BF16),
            pltpu.VMEM((NY - 1, NL, pair, half), BF16),
            pltpu.VMEM((NL - 1, pair, half), BF16),
            pltpu.VMEM((NL - 1, pair, half), BF16),
            pltpu.VMEM((2, own, half), F32),
            pltpu.VMEM((own, half), F32),
            pltpu.VMEM((NZ, NX, ff, tok), F32),
            pltpu.VMEM((NX - 1, NZ, ff, tok), BF16),
            pltpu.VMEM((NX - 1, NZ, ff, tok), BF16),
            pltpu.VMEM((NZ - 1, ff, tok), BF16),
            pltpu.VMEM((NZ - 1, ff, tok), BF16),
            pltpu.SemaphoreType.DMA((COPIES,)),
            pltpu.SemaphoreType.DMA((COPIES,)),
        ],
        compiler_params=pltpu.CompilerParams(
            collective_id=0, has_side_effects=True, vmem_limit_bytes=56 * 1024 * 1024
        ),
        cost_estimate=pl.CostEstimate(
            flops=6 * tokens * ff * feat, bytes_accessed=4 * ff * feat, transcendentals=tok * ff
        ),
    )(gate_pre, up_pre, down_weight, out_grad, noised.reshape(1, own))


def solution(mesh):
    return jax.shard_map(
        body,
        mesh=mesh,
        in_specs=(P("row", "col"), P("row", "col"), P("col", "row"), P("col", "row"), P("col")),
        out_specs=(P("col", "row"), P("row", "col"), P("row", "col"), P("col", "row")),
        check_vma=False,
    )
```

time: 832 us -> 86.2 us (0.10)
  waiting for transfers between devices: 648 us -> 0 us
  blocking collectives: 144 us -> 0 us
  Pallas kernels: 0 us -> 77.7 us
  between operations: 14.5 us -> 0.66 us
  matrix products: 11 us -> 0 us
    reduce_scatter x1 -> x0, waiting for transfers between devices: 278 us -> none  [body(): lax.psum_scatter(jnp.dot(rows, down_weight, preferred_element_type=jnp.fl...]
    all_gather x2 -> x0, waiting for transfers between devices: 200 us -> none  [the longest x1 122 us: body(): scaled = lax.all_gather(local_scaled, 'col', axis=0, tiled=True)]
    unnamed x5 -> x0, waiting for transfers between devices: 170 us -> none
    psum x1 -> x0, blocking collectives: 144 us -> none  [body(): count = lax.psum(jnp.sum(local_flags), 'col')]
    pallas_call x0 -> x1, Pallas kernels: none -> 77.7 us  [body(): pl.pallas_call(kernel, out_shape=(jax.ShapeDtypeStruct((own, feat), BF16)...]
    dot_general x3 -> x0, matrix products: 11 us -> none  [the longest x1 4.86 us: body(): jnp.dot(rows, down_weight, preferred_element_type=jnp.float32)]
  transfers between devices with their start and end apart: 4 -> 0, of which waited for: 4 -> 0; matrix products, arithmetic and copies ran while one was open for 0% -> 0% of each run, Pallas kernels for 0% -> 0%
where the time goes in v1:
time: 86.2 us; the launch traced here: 85.8 us
  Pallas kernels  77.7 us (90%)
  local copies, waits for them, and re-layouts  7.48 us (9%)
    pallas_call x1, Pallas kernels, body(): pl.pallas_call(kernel, out_shape=(jax.ShapeDtypeStruct((own, feat), BF16)...  77.7 us
    unnamed x10, local copies, waits for them, and re-layouts  5.04 us
    pallas_call x2, local copies, waits for them, and re-layouts, body(): pl.pallas_call(kernel, out_shape=(jax.ShapeDtypeStruct((own, feat), BF16)...  2.45 us

profile of v1, /device:TPU:1, one launch (start us, length us, event | category | flops | bytes accessed | tf_op | source)
XLA Modules:
  0.0 85.8 jit_solution(13990383353968211408)
XLA Ops:
  0.6 0.0 copy-start.1
  0.6 1.7 %copy.9.gate_ref = bf16[128,416]{1,0:T(8,128)(2,1)} copy(bf16[128,416]{0,1:T(8,128)(2,1)} %param.5) | data formatting | bytes 212992 | tf_op args[0]
  2.3 0.0 copy-done.1
  2.3 0.8 copy.10.up_ref
  3.1 77.7 %shard_map.84 = (bf16[24,768]{1,0:T(8,128)(2,1)}, bf16[128,416]{1,0:T(8,128)(2,1)}, bf16[128,416]{1,0:T(8,128)(2,1)}, bf16[416,768]{1,0:T(8,128)(2,1)}) custom-call(bf16[128,416]{1,0:T(8,128)(2,1)} %copy.9.gate_ref, bf16[128,416]{1,0:T(8,128)(2,1)} %copy.10.up_ref, bf16[416,768]{1,0:T(8,128)(2,1)} %w_ref.1, bf16[24,768]{1,0:T(8,128)(2,1)} %og_ref.1, ...), custom_call_target="tpu_custom_call" | custom-call | flops 2944401408 | bytes 1277952 | tf_op jit(solution)/shard_map/pallas_call | solution.py:433
  80.8 0.0 copy-start
  80.8 1.7 %copy.11 = bf16[128,416]{0,1:T(8,128)(2,1)} copy(bf16[128,416]{1,0:T(8,128)(2,1)} %get-tuple-element.5) | data formatting | bytes 212992 | tf_op jit(solution)/shard_map/pallas_call | solution.py:433
  82.5 0.0 copy-done
  82.5 0.0 copy-start.2
  82.5 0.8 copy.12
  83.3 0.0 copy-done.2
  83.3 0.6 copy.15
  83.9 2.0 %copy.16 = bf16[416,768]{1,0:T(8,128)(2,1)} copy(bf16[416,768]{1,0:T(8,128)(2,1)} %get-tuple-element.15) | data formatting | bytes 1277952
Async XLA Ops:
  0.6 1.7 %copy-start.1 = (bf16[128,416]{0,1:T(8,128)(2,1)S(1)}, bf16[128,416]{0,1:T(8,128)(2,1)}, u32[]{:S(2)}) copy-start(bf16[128,416]{0,1:T(8,128)(2,1)} %param.6) | copy-start | bytes 319492
  80.8 1.7 %copy-start = (bf16[128,416]{1,0:T(8,128)(2,1)S(1)}, bf16[128,416]{1,0:T(8,128)(2,1)}, u32[]{:S(2)}) copy-start(bf16[128,416]{1,0:T(8,128)(2,1)} %get-tuple-element.6) | copy-start | bytes 319492
  82.5 0.8 copy-start.2

commit v2 on v0

v2 whole, which is shorter than its diff:
```python
import jax
import jax.numpy as jnp
from jax import lax
from jax.experimental import pallas as pl
from jax.experimental.pallas import tpu as pltpu
from jax.sharding import PartitionSpec as P

MESH = pl.DeviceIdType.MESH
F32 = jnp.float32
BF16 = jnp.bfloat16
NZ, NX, NY, NL = 3, 4, 8, 4
COPIES = 200


def kernel(
    gate_hbm, up_hbm, w_hbm, og_hbm, noised_hbm,
    lo_ref, gg_ref, ug_ref, wg_ref,
    gate_ref, up_ref, w_ref, og_ref, noised_ref,
    x0_send, x0_recv, s_buf, ht, cl_send, cl_recv, cy_own, cy_recv,
    po, ps, pr, y_send, y_recv, l_send, l_recv,
    x_send, x_recv, z_send, z_recv,
    in_sem, zl_sem, fin_sem, send_sem, recv_sem,
):
    ff, tok = gate_ref.shape
    own_tok, feat = og_ref.shape
    half = feat // 2
    pair = 2 * own_tok
    tokens = tok * NZ * NX

    loads = [
        pltpu.make_async_copy(src, dst, in_sem.at[i])
        for i, (src, dst) in enumerate([
            (og_hbm, og_ref), (noised_hbm, noised_ref), (gate_hbm, gate_ref),
            (up_hbm, up_ref), (w_hbm, w_ref),
        ])
    ]
    for load in loads:
        load.start()

    row, col = lax.axis_index("row"), lax.axis_index("col")
    zh, x = row // NX, row % NX
    c, chip = col % 2, col // 2
    y, zl = chip // NL, chip % NL
    first = c == 0
    sgn = 1 - 2 * c

    def at(zh_=zh, x_=x, y_=y, zl_=zl, c_=c):
        return (zh_ * NX + x_, (y_ * NL + zl_) * 2 + c_)

    def xi(d):
        return (x + sgn * d + 2 * NX) % NX

    def yi(d):
        return (y + sgn * d + 2 * NY) % NY

    sibling = at(c_=1 - c)
    x_at = [at(x_=xi(d)) for d in range(NX)]
    y_way = (at(y_=yi(1)), at(y_=yi(-1)))
    zl_at = [at(zl_=(zl + k) % NL) for k in range(NL)]
    zh_at = [at(zh_=(zh + k) % NZ) for k in range(NZ)]

    started = []

    def send(src, dst, device, arrived=None):
        i = len(started)
        copy = pltpu.make_async_remote_copy(
            src_ref=src, dst_ref=dst, send_sem=send_sem.at[i],
            recv_sem=recv_sem.at[i] if arrived is None else arrived,
            device_id=device, device_id_type=MESH,
        )
        copy.start()
        started.append(copy)
        return copy

    barrier = pltpu.get_barrier_semaphore()
    partners = [sibling, *y_way] + x_at[1:] + zl_at[1:] + zh_at[1:]
    partners += [at(zl_=(zl + k) % NL, c_=1 - c) for k in range(1, NL)]
    for partner in partners:
        pl.semaphore_signal(barrier, inc=1, device_id=partner, device_id_type=MESH)

    loads[0].wait()
    loads[1].wait()
    flags_row = noised_ref[...].astype(F32)
    i0 = lax.broadcasted_iota(jnp.int32, (own_tok, own_tok), 0)
    i1 = lax.broadcasted_iota(jnp.int32, (own_tok, own_tok), 1)
    flags = jnp.sum(
        jnp.where(i0 == i1, jnp.broadcast_to(flags_row, (own_tok, own_tok)), 0.0),
        axis=1, keepdims=True,
    )
    masked = og_ref[...].astype(F32) * flags
    own_count = jnp.sum(jnp.broadcast_to(flags_row, (8, own_tok)), axis=1, keepdims=True)
    lo, hi = masked[:, :half], masked[:, half:]
    x0_send[0:own_tok, :] = jnp.where(first, hi, lo)
    x0_send[own_tok:own_tok + 8, :] = jnp.broadcast_to(own_count, (8, half))

    loads[2].wait()
    loads[3].wait()

    def parts():
        gate = gate_ref[...].astype(F32)
        sigma = jax.nn.sigmoid(gate)
        return gate, up_ref[...].astype(F32), sigma, gate * sigma

    _, upper, _, silu = parts()
    ht[row] = (silu * upper).astype(BF16)

    up = zl // 2

    def near(j):
        rising = (j - 1) + 1 - (zl + 3 - (j - 1)) // 4
        falling = 3 - ((j - 1) + 1 - (3 - zl + 3 - (j - 1)) // 4)
        return (1 - up) * rising + up * falling

    cuts, r0 = [], 0
    for n in (112, 112, 112, 80):
        cuts.append((r0, n))
        r0 += n

    def block(k, d):
        return ((zh - k + NZ) % NZ) * NX + xi(d)

    pl.semaphore_wait(barrier, len(partners))
    x0 = send(x0_send, x0_recv, sibling)
    z_cp = []

    def z_start(q):
        b = ht.at[row, pl.ds(*cuts[q])]
        z_cp.append([send(b, b, zh_at[k]) for k in (1, 2)])

    z_start(0)

    x_cp = {}

    def x_spread(k, q, a, n):
        b = ht.at[block(k, 0), pl.ds(a, n)]
        for d in (2, 1, 3):
            x_cp[k, q, d] = send(b, b, x_at[d])

    x_spread(0, 0, 0, ff)

    def z_arrive(q):
        for k in (1, 2):
            z_cp[q][k - 1].wait_recv()
            x_spread(k, q, *cuts[q])

    def x_arrive(k, d):
        for q in range(len(cuts) if k else 1):
            x_cp[k, q, d].wait_recv()

    x0.wait_recv()
    got = x0_recv[0:own_tok, :]
    cols = pl.ds(pl.multiple_of(c * half, 128), half)

    def s_block(y_, l_, n=1):
        return s_buf.at[pl.ds(pl.multiple_of((y_ * NL + l_) * pair, 16), n * pair), cols]

    kept = jnp.where(first, og_ref[:, :half].astype(F32), og_ref[:, half:].astype(F32)) * flags
    s_block(y, zl)[...] = jnp.concatenate(
        [jnp.where(first, kept, got), jnp.where(first, got, kept)], axis=0
    ).astype(BF16)
    cl_send[...] = own_count + x0_recv[own_tok:own_tok + 8, 0:128]
    own = s_block(y, zl)
    l_cp = [send(own, own, zl_at[k], zl_sem.at[zl]) for k in range(1, NL)]

    def zl_arrive(j):
        b = s_block(y, near(j))
        pltpu.make_async_remote_copy(
            src_ref=b, dst_ref=b, send_sem=send_sem.at[0], recv_sem=zl_sem.at[near(j)],
            device_id=sibling, device_id_type=MESH,
        ).wait_recv()

    def of_chip(j):
        return near(j) if j else zl

    y_cp = {}

    def y_start(k, way, step):
        sign = 1 if way == 0 else -1
        b = s_block(yi(-sign * step), of_chip(k))
        if step:
            y_cp[k, way, step - 1].wait_recv()
        y_cp[k, way, step] = send(b, b, y_way[way])

    sib_cp = {}

    def to_sibling(d):
        b = s_block(yi(d), 0, NL)
        sib_cp[d % NY] = send(b, b, sibling)

    def chunk_to_sibling(k, d):
        b = s_block(yi(d), of_chip(k))
        sib_cp[d % NY, k] = send(b, b, sibling)

    cy_cp = {}

    def cy_start(way, step):
        if step:
            cy_cp[way, step - 1].wait_recv()
        slot = way * 4 + step
        src = cy_recv.at[slot - 1] if step else cy_own
        cy_cp[way, step] = send(src, cy_recv.at[slot], y_way[way])

    y_start(0, 0, 0)
    y_start(0, 1, 0)
    cl_cp = [send(cl_send, cl_recv.at[k - 1], zl_at[k]) for k in range(1, NL)]
    for q in range(1, len(cuts)):
        z_start(q)

    p_cp = {}

    def p_block(k, d):
        b = block(k, d)
        rows = pl.ds(pl.multiple_of(b * tok, tok), tok)
        out = jnp.dot(jnp.transpose(ht[b]), w_ref[...], preferred_element_type=F32)
        po[rows, :] = jnp.where(first, out[:, :half], out[:, half:])
        ps[rows, :] = jnp.where(first, out[:, half:], out[:, :half]).astype(BF16)
        p_cp[k, d] = send(ps.at[rows], pr.at[rows], sibling)

    loads[4].wait()
    p_block(0, 0)
    y_start(0, 0, 1)
    y_start(0, 1, 1)
    for k in range(1, NL):
        zl_arrive(k)
        y_start(k, 0, 0)
        y_start(k, 1, 0)
    z_arrive(0)
    to_sibling(0)
    total = cl_send[...]
    for k in range(1, NL):
        cl_cp[k - 1].wait_recv()
        total = total + cl_recv[k - 1]
    cy_own[...] = total
    cy_start(0, 0)
    cy_start(1, 0)
    y_start(0, 0, 2)
    y_start(0, 1, 2)
    z_arrive(1)
    for k in range(1, NL):
        y_start(k, 0, 1)
        y_start(k, 1, 1)
    to_sibling(-1)
    to_sibling(1)
    y_start(0, 0, 3)
    cy_start(0, 1)
    cy_start(1, 1)
    for d in (1, 3, 2):
        x_arrive(0, d)
        p_block(0, NX - d)
    z_arrive(2)
    for k in range(1, NL):
        y_start(k, 0, 2)
        y_start(k, 1, 2)
    to_sibling(-2)
    to_sibling(2)
    cy_start(0, 2)
    cy_start(1, 2)
    z_arrive(3)
    p_block(1, 0)
    p_block(2, 0)
    for k in range(NL):
        if k:
            y_start(k, 0, 3)
        y_cp[k, 1, 2].wait_recv()
        chunk_to_sibling(k, -3)
        chunk_to_sibling(k, 3)
    cy_start(0, 3)

    span = NX * tok
    pieces = {(k, q): cut for k in (1, 2) for q, cut in enumerate(cuts)}
    pieces[0, 0] = (0, ff)
    g_cp = {}

    def g_start(k, q):
        a, n = pieces[k, q]
        rows = s_buf[pl.ds(pl.multiple_of((zh + k) % NZ * span, span), span), :]
        out = lax.dot_general(
            w_ref[a:a + n, :], rows, (((1,), (1,)), ((), ())), preferred_element_type=F32
        ).astype(BF16)
        for x_ in range(NX):
            d = (sgn * (x_ - x) + 2 * NX) % NX
            x_send[d, k, a:a + n, :] = out[:, x_ * tok:(x_ + 1) * tok]
        for d in (2, 1, 3):
            g_cp[k, q, d] = send(
                x_send.at[d, k, pl.ds(a, n)], x_recv.at[d - 1, k, pl.ds(a, n)], x_at[d]
            )

    zr_cp = []

    def g_sum(k, q):
        a, n = pieces[k, q]
        value = x_send[0, k, a:a + n, :].astype(F32)
        for d in (1, 3, 2):
            g_cp[k, q, d].wait_recv()
            value = value + x_recv[d - 1, k, a:a + n, :].astype(F32)
        return value

    def g_last(q):
        for k in (1, 2):
            a, n = pieces[k, q]
            z_send[k - 1, a:a + n, :] = g_sum(k, q).astype(BF16)
            zr_cp.append(send(
                z_send.at[k - 1, pl.ds(a, n)], z_recv.at[k - 1, pl.ds(a, n)], zh_at[k]
            ))

    ry_cp = {}

    def p_sum(d, j):
        to = near(3 - j) if j < NL - 1 else zl
        rows = pl.ds(pl.multiple_of((yi(d) * NL + to) * pair, 16), pair)
        return po[rows, :] + pr[rows, :].astype(F32)

    def ry_send(way, step, j):
        d = 4 - step if way == 0 else step - 3
        slot = way * 4 + step
        value = p_sum(d, j)
        if step:
            ry_cp[way, step - 1, j].wait_recv()
            value = value + y_recv[slot - 1, j].astype(F32)
        y_send[slot, j] = value.astype(BF16)
        ry_cp[way, step, j] = send(y_send.at[slot, j], y_recv.at[slot, j], y_way[way])

    def ry_both(step):
        for j in range(NL):
            ry_send(0, step, j)
            if step < 3:
                ry_send(1, step, j)

    for d in (1, 3, 2):
        for k in (1, 2):
            x_arrive(k, d)
            p_block(k, NX - d)
    for k in range(NL):
        y_cp[k, 0, 3].wait_recv()
        chunk_to_sibling(k, 4)
    for copy in p_cp.values():
        copy.wait_recv()
    ry_both(0)
    for copy in sib_cp.values():
        copy.wait_recv()
    for q in range(len(cuts)):
        g_start(1, q)
        g_start(2, q)
    ry_both(1)
    g_start(0, 0)

    for way in range(2):
        cy_cp[way, 3 - way].wait_recv()
    count = cy_own[...]
    for slot in range(7):
        count = count + cy_recv[slot]
    scale = tokens / count

    nb = 256
    scale_w = jnp.broadcast_to(scale[0:1, 0:1], (1, nb))

    def w_product(j):
        acc = jnp.zeros((ff, nb), F32)
        for i in range(NZ * NX // 2):
            acc = acc + jnp.dot(
                jnp.concatenate([ht[2 * i], ht[2 * i + 1]], axis=1),
                s_buf[2 * tok * i:2 * tok * (i + 1), j * nb:(j + 1) * nb],
                preferred_element_type=F32,
            )
        wg_ref[:, j * nb:(j + 1) * nb] = (acc * scale_w).astype(BF16)

    g_last(0)
    ry_both(2)
    w_product(0)
    g_last(1)
    ry_both(3)
    g_last(2)
    w_product(1)

    def piece(c_):
        return pl.ds(pl.multiple_of(16 * c_, 16), 32)

    def last_slot(zl_, c_):
        return l_recv.at[zl_ * 2 + c_], fin_sem.at[zl_ * 2 + c_]

    for j in range(NL):
        ry_cp[0, 3, j].wait_recv()
        ry_cp[1, 2, j].wait_recv()
        out = p_sum(0, j) + y_recv[3, j].astype(F32) + y_recv[6, j].astype(F32)
        l_send[j] = out.astype(BF16)
        dst, arrived = last_slot(zl, c)
        if j < NL - 1:
            for c_ in range(2):
                send(l_send.at[j, pl.ds(16 * c_, 32)], dst, at(zl_=near(3 - j), c_=c_), arrived)
        else:
            send(l_send.at[j, piece(1 - c)], dst, sibling, arrived)
    g_last(3)
    tail = g_sum(0, 0)
    w_product(2)

    def arrived_piece(zl_, c_):
        dst, arrived = last_slot(zl_, c_)
        pltpu.make_async_remote_copy(
            src_ref=dst, dst_ref=dst, send_sem=send_sem.at[0], recv_sem=arrived,
            device_id=sibling, device_id_type=MESH,
        ).wait_recv()
        return l_recv[zl_ * 2 + c_].astype(F32)

    mine = jnp.where(first, out[0:32], out[16:48])
    theirs = arrived_piece(zl, 1 - c)
    for j in range(1, NL):
        mine = mine + arrived_piece(near(j), c)
        theirs = theirs + arrived_piece(near(j), 1 - c)
    mine = jnp.where(first, mine[0:own_tok], mine[8:8 + own_tok])
    theirs = jnp.where(first, theirs[0:own_tok], theirs[8:8 + own_tok])
    lo_ref[:, :half] = jnp.where(first, mine, theirs).astype(BF16)
    lo_ref[:, half:] = jnp.where(first, theirs, mine).astype(BF16)

    for copy in zr_cp:
        copy.wait_recv()
    grad = (tail + z_recv[0].astype(F32) + z_recv[1].astype(F32)) * scale[0:1, :]
    gate, upper, sigma, silu = parts()
    gg_ref[...] = (grad * upper * (sigma * (1.0 + gate * (1.0 - sigma)))).astype(BF16)
    ug_ref[...] = (grad * silu).astype(BF16)

    for copy in started:
        copy.wait_send()


def write_kernel(*refs):
    n = len(refs) // 2
    sems = refs[-1]
    copies = [pltpu.make_async_copy(refs[i], refs[n + i], sems.at[i]) for i in range(n)]
    for copy in copies:
        copy.start()
    for copy in copies:
        copy.wait()


def written(arrays):
    return pl.pallas_call(
        write_kernel,
        out_shape=tuple(jax.ShapeDtypeStruct(a.shape, a.dtype) for a in arrays),
        in_specs=[pl.BlockSpec(memory_space=pltpu.VMEM)] * len(arrays),
        out_specs=(pl.BlockSpec(memory_space=pl.ANY),) * len(arrays),
        scratch_shapes=[pltpu.SemaphoreType.DMA((len(arrays),))],
        compiler_params=pltpu.CompilerParams(vmem_limit_bytes=4 * 1024 * 1024),
    )(*arrays)


def body(gate_pre, up_pre, down_weight, out_grad, noised):
    tok, ff = gate_pre.shape
    own, feat = out_grad.shape
    half, pair, tokens = feat // 2, 2 * own, tok * NZ * NX
    vmem = pl.BlockSpec(memory_space=pltpu.VMEM)
    layer_out, gate_grad, up_grad, weight_grad = written(pl.pallas_call(
        kernel,
        out_shape=(
            pltpu.VMEM((own, feat), BF16),
            pltpu.VMEM((ff, tok), BF16),
            pltpu.VMEM((ff, tok), BF16),
            pltpu.VMEM((ff, feat), BF16),
        ),
        in_specs=[pl.BlockSpec(memory_space=pl.ANY)] * 5,
        out_specs=(vmem,) * 4,
        scratch_shapes=[
            pltpu.VMEM((ff, tok), BF16),
            pltpu.VMEM((ff, tok), BF16),
            pltpu.VMEM((ff, feat), BF16),
            pltpu.VMEM((own, feat), BF16),
            pltpu.VMEM((1, own), jnp.int32),
            pltpu.VMEM((own + 8, half), F32),
            pltpu.VMEM((own + 8, half), F32),
            pltpu.VMEM((tokens, feat), BF16),
            pltpu.VMEM((NZ * NX, ff, tok), BF16),
            pltpu.VMEM((8, 128), F32),
            pltpu.VMEM((NL - 1, 8, 128), F32),
            pltpu.VMEM((8, 128), F32),
            pltpu.VMEM((NY - 1, 8, 128), F32),
            pltpu.VMEM((tokens, half), F32),
            pltpu.VMEM((tokens, half), BF16),
            pltpu.VMEM((tokens, half), BF16),
            pltpu.VMEM((NY - 1, NL, pair, half), BF16),
            pltpu.VMEM((NY - 1, NL, pair, half), BF16),
            pltpu.VMEM((NL, pair, half), BF16),
            pltpu.VMEM((2 * NL, 32, half), BF16),
            pltpu.VMEM((NX, NZ, ff, tok), BF16),
            pltpu.VMEM((NX - 1, NZ, ff, tok), BF16),
            pltpu.VMEM((NZ - 1, ff, tok), BF16),
            pltpu.VMEM((NZ - 1, ff, tok), BF16),
            pltpu.SemaphoreType.DMA((5,)),
            pltpu.SemaphoreType.DMA((NL,)),
            pltpu.SemaphoreType.DMA((2 * NL,)),
            pltpu.SemaphoreType.DMA((COPIES,)),
            pltpu.SemaphoreType.DMA((COPIES,)),
        ],
        compiler_params=pltpu.CompilerParams(
            collective_id=0, has_side_effects=True, vmem_limit_bytes=56 * 1024 * 1024
        ),
        cost_estimate=pl.CostEstimate(
            flops=6 * tokens * ff * feat, bytes_accessed=4 * ff * feat, transcendentals=tok * ff
        ),
    )(gate_pre.T, up_pre.T, down_weight, out_grad, noised.reshape(1, own)))
    return layer_out, gate_grad.T, up_grad.T, weight_grad


def solution(mesh):
    return jax.shard_map(
        body,
        mesh=mesh,
        in_specs=(P("row", "col"), P("row", "col"), P("col", "row"), P("col", "row"), P("col")),
        out_specs=(P("col", "row"), P("row", "col"), P("row", "col"), P("col", "row")),
        check_vma=False,
    )
```

time: 832 us -> 74 us (0.09)
  waiting for transfers between devices: 648 us -> 0 us
  blocking collectives: 144 us -> 0 us
  Pallas kernels: 0 us -> 73.2 us
  between operations: 14.5 us -> 0.64 us
  matrix products: 11 us -> 0 us
    reduce_scatter x1 -> x0, waiting for transfers between devices: 278 us -> none  [body(): lax.psum_scatter(jnp.dot(rows, down_weight, preferred_element_type=jnp.fl...]
    all_gather x2 -> x0, waiting for transfers between devices: 200 us -> none  [the longest x1 122 us: body(): scaled = lax.all_gather(local_scaled, 'col', axis=0, tiled=True)]
    unnamed x5 -> x0, waiting for transfers between devices: 170 us -> none
    psum x1 -> x0, blocking collectives: 144 us -> none  [body(): count = lax.psum(jnp.sum(local_flags), 'col')]
    pallas_call x0 -> x2, Pallas kernels: none -> 73.2 us  [the longest x1 72.3 us: body(): pl.pallas_call(kernel, out_shape=(pltpu.VMEM((own, feat), BF16), pltpu.VM...]
    dot_general x3 -> x0, matrix products: 11 us -> none  [the longest x1 4.86 us: body(): jnp.dot(rows, down_weight, preferred_element_type=jnp.float32)]
  transfers between devices with their start and end apart: 4 -> 0, of which waited for: 4 -> 0; matrix products, arithmetic and copies ran while one was open for 0% -> 0% of each run, Pallas kernels for 0% -> 0%
where the time goes in v2:
time: 74 us; the launch traced here: 73.8 us
  Pallas kernels  73.2 us (99%)
    pallas_call x1, Pallas kernels, body(): pl.pallas_call(kernel, out_shape=(pltpu.VMEM((own, feat), BF16), pltpu.VM...  72.3 us

profile of v2, /device:TPU:1, one launch (start us, length us, event | category | flops | bytes accessed | tf_op | source)
XLA Modules:
  0.0 73.8 jit_solution(12590168491604570307)
XLA Ops:
  0.6 72.3 %shard_map.84 = (bf16[24,768]{1,0:T(8,128)(2,1)S(1)}, bf16[416,128]{1,0:T(8,128)(2,1)S(1)}, bf16[416,128]{1,0:T(8,128)(2,1)S(1)}, bf16[416,768]{1,0:T(8,128)(2,1)S(1)}) custom-call(bf16[416,128]{1,0:T(8,128)(2,1)} %bitcast.5, bf16[416,128]{1,0:T(8,128)(2,1)} %bitcast.6, bf16[416,768]{1,0:T(8,128)(2,1)} %w_hbm.1, bf16[24,768]{1,0:T(8,128)(2,1)} %og_hbm.1, ...), custom_call_target="tpu_custom_call" | custom-call | flops 2944401408 | bytes 1277952 | tf_op jit(solution)/shard_map/pallas_call | solution.py:451
  72.9 1.0 %shard_map.85 = (bf16[24,768]{1,0:T(8,128)(2,1)}, bf16[416,128]{1,0:T(8,128)(2,1)}, bf16[416,128]{1,0:T(8,128)(2,1)}, bf16[416,768]{1,0:T(8,128)(2,1)}) custom-call(bf16[24,768]{1,0:T(8,128)(2,1)S(1)} %get-tuple-element.12.refs_0_, bf16[416,128]{1,0:T(8,128)(2,1)S(1)} %get-tuple-element.13.refs_1_, bf16[416,128]{1,0:T(8,128)(2,1)S(1)} %get-tuple-element.14.refs_2_, ...), custom_call_target="tpu_custom_call" | custom-call | tf_op jit(solution)/shard_map/pallas_call | solution.py:436

commit v3 on v2

--- a/solution.py
+++ b/solution.py
@@ -18,7 +18,7 @@
     gate_ref, up_ref, w_ref, og_ref, noised_ref,
     x0_send, x0_recv, s_buf, ht, cl_send, cl_recv, cy_own, cy_recv,
     po, ps, pr, y_send, y_recv, l_send, l_recv,
-    x_send, x_recv, z_send, z_recv,
+    x_send, x_recv, x_pass, z_send, z_recv,
     in_sem, zl_sem, fin_sem, send_sem, recv_sem,
 ):
     ff, tok = gate_ref.shape
@@ -203,8 +203,6 @@
     y_start(0, 0, 0)
     y_start(0, 1, 0)
     cl_cp = [send(cl_send, cl_recv.at[k - 1], zl_at[k]) for k in range(1, NL)]
-    for q in range(1, len(cuts)):
-        z_start(q)
 
     p_cp = {}
 
@@ -222,6 +220,9 @@
     y_start(0, 1, 1)
     for k in range(1, NL):
         zl_arrive(k)
+        if k == NL - 1:
+            for q in range(1, len(cuts)):
+                z_start(q)
         y_start(k, 0, 0)
         y_start(k, 1, 0)
     z_arrive(0)
@@ -280,19 +281,32 @@
         for x_ in range(NX):
             d = (sgn * (x_ - x) + 2 * NX) % NX
             x_send[d, k, a:a + n, :] = out[:, x_ * tok:(x_ + 1) * tok]
-        for d in (2, 1, 3):
-            g_cp[k, q, d] = send(
-                x_send.at[d, k, pl.ds(a, n)], x_recv.at[d - 1, k, pl.ds(a, n)], x_at[d]
+        for slot, d, way in ((0, 2, 1), (2, 3, 3)):
+            g_cp[k, q, slot] = send(
+                x_send.at[d, k, pl.ds(a, n)], x_recv.at[slot, k, pl.ds(a, n)], x_at[way]
             )
+
+    def g_pass(k, q):
+        a, n = pieces[k, q]
+        g_cp[k, q, 0].wait_recv()
+        value = x_send[1, k, a:a + n, :].astype(F32) + x_recv[0, k, a:a + n, :].astype(F32)
+        x_pass[k, a:a + n, :] = value.astype(BF16)
+        g_cp[k, q, 1] = send(
+            x_pass.at[k, pl.ds(a, n)], x_recv.at[1, k, pl.ds(a, n)], x_at[1]
+        )
+
+    def g_both(q):
+        g_pass(1, q)
+        g_pass(2, q)
 
     zr_cp = []
 
     def g_sum(k, q):
         a, n = pieces[k, q]
         value = x_send[0, k, a:a + n, :].astype(F32)
-        for d in (1, 3, 2):
-            g_cp[k, q, d].wait_recv()
-            value = value + x_recv[d - 1, k, a:a + n, :].astype(F32)
+        for slot in (2, 1):
+            g_cp[k, q, slot].wait_recv()
+            value = value + x_recv[slot, k, a:a + n, :].astype(F32)
         return value
 
     def g_last(q):
@@ -342,7 +356,12 @@
         g_start(1, q)
         g_start(2, q)
     ry_both(1)
+    g_both(0)
+    g_both(1)
     g_start(0, 0)
+    g_last(0)
+    g_both(2)
+    g_last(1)
 
     for way in range(2):
         cy_cp[way, 3 - way].wait_recv()
@@ -364,13 +383,12 @@
             )
         wg_ref[:, j * nb:(j + 1) * nb] = (acc * scale_w).astype(BF16)
 
-    g_last(0)
     ry_both(2)
+    g_both(3)
+    g_last(2)
     w_product(0)
-    g_last(1)
     ry_both(3)
-    g_last(2)
-    w_product(1)
+    g_last(3)
 
     def piece(c_):
         return pl.ds(pl.multiple_of(16 * c_, 16), 32)
@@ -389,7 +407,8 @@
                 send(l_send.at[j, pl.ds(16 * c_, 32)], dst, at(zl_=near(3 - j), c_=c_), arrived)
         else:
             send(l_send.at[j, piece(1 - c)], dst, sibling, arrived)
-    g_last(3)
+    g_pass(0, 0)
+    w_product(1)
     tail = g_sum(0, 0)
     w_product(2)
 
@@ -481,6 +500,7 @@
             pltpu.VMEM((2 * NL, 32, half), BF16),
             pltpu.VMEM((NX, NZ, ff, tok), BF16),
             pltpu.VMEM((NX - 1, NZ, ff, tok), BF16),
+            pltpu.VMEM((NZ, ff, tok), BF16),
             pltpu.VMEM((NZ - 1, ff, tok), BF16),
             pltpu.VMEM((NZ - 1, ff, tok), BF16),
             pltpu.SemaphoreType.DMA((5,)),

time: 74 us -> 74.2 us (level)
  no operation moved by 1% of the time
where the time goes in v3:
time: 74.2 us; the launch traced here: 74 us
  Pallas kernels  73.4 us (99%)
    pallas_call x1, Pallas kernels, body(): pl.pallas_call(kernel, out_shape=(pltpu.VMEM((own, feat), BF16), pltpu.VM...  72.5 us

profile of v3, /device:TPU:1, one launch (start us, length us, event | category | flops | bytes accessed | tf_op | source)
XLA Modules:
  0.0 74.0 jit_solution(3631881945600196805)
XLA Ops:
  0.6 72.5 %shard_map.84 = (bf16[24,768]{1,0:T(8,128)(2,1)S(1)}, bf16[416,128]{1,0:T(8,128)(2,1)S(1)}, bf16[416,128]{1,0:T(8,128)(2,1)S(1)}, bf16[416,768]{1,0:T(8,128)(2,1)S(1)}) custom-call(bf16[416,128]{1,0:T(8,128)(2,1)} %bitcast.5, bf16[416,128]{1,0:T(8,128)(2,1)} %bitcast.6, bf16[416,768]{1,0:T(8,128)(2,1)} %w_hbm.1, bf16[24,768]{1,0:T(8,128)(2,1)} %og_hbm.1, ...), custom_call_target="tpu_custom_call" | custom-call | flops 2944401408 | bytes 1277952 | tf_op jit(solution)/shard_map/pallas_call | solution.py:470
  73.1 1.0 %shard_map.85 = (bf16[24,768]{1,0:T(8,128)(2,1)}, bf16[416,128]{1,0:T(8,128)(2,1)}, bf16[416,128]{1,0:T(8,128)(2,1)}, bf16[416,768]{1,0:T(8,128)(2,1)}) custom-call(bf16[24,768]{1,0:T(8,128)(2,1)S(1)} %get-tuple-element.12.refs_0_, bf16[416,128]{1,0:T(8,128)(2,1)S(1)} %get-tuple-element.13.refs_1_, bf16[416,128]{1,0:T(8,128)(2,1)S(1)} %get-tuple-element.14.refs_2_, ...), custom_call_target="tpu_custom_call" | custom-call | tf_op jit(solution)/shard_map/pallas_call | solution.py:455
